TPU v7x, 128 devices: a whole 4x4x4 slice. The times are simulated.
128 devices in a mesh: aa: 16 (over y, x_hi, core), ba: 8 (over x_lo, z).
Axes of the slice: x: 4 (x_hi: 2, x_lo: 2; x = x_hi * 2 + x_lo), y: 4, z: 4, core: 2. Of those that a mesh axis runs over, the one named last changes fastest.
Arguments:
- features: bfloat16 [65536, 128], P(('aa', 'ba')), may hold values from -6 to 6
- tile_values: bfloat16 [16384, 128, 128], P(('aa', 'ba')), may hold values from -0.125 to 0.125
- tile_row: int32 [16384], P(('aa', 'ba')), may hold values from -1 to 511, as said below
- tile_col: int32 [16384], P(('aa', 'ba')), may hold values from -1 to 511, as said below
- weight_one: bfloat16 [128, 1024], replicated, may hold values from -0.5 to 0.5
- bias_one: float32 [1024], replicated, may hold values from -3 to 3
- weight_two: bfloat16 [1024, 1024], replicated, may hold values from -0.1875 to 0.1875
Outputs:
- layer_two: bfloat16 [65536, 1024], P('aa', 'ba')
Inputs may be any that keep to these rules, and one draw needn't show every extreme that they name: Slot s belongs to device s // 128, devices in the order of aa then ba. A live slot of device (a, b) names a row block from a * 32 to a * 32 + 31; an empty slot holds -1 in tile_row and in tile_col. A device's live slots come first among its slots; some device has all 128 slots live. Tiles may repeat. `tile_col`: A live slot of device (a, b) names a column block c with (c // 4) % (number of ba devices) == b.
All inputs are finite; a program needn't handle non-finite values.
Results may differ from a plain program's by a relative error of at most 0.0063.
Values may be sent and summed in bfloat16 or wider, within the bound.
A program may use at most 192 MiB of HBM per device.

v0:
```python
import jax
import jax.numpy as jnp
from jax import lax
from jax.sharding import PartitionSpec as P


def local_columns(tile_col, dev_blocks, ba_count):
    clamped = jnp.maximum(tile_col, 0)
    return clamped // (dev_blocks * ba_count) * dev_blocks + clamped % dev_blocks


def local_rows(tile_row, range_blocks):
    return jnp.where(tile_row < 0, -1, tile_row % range_blocks)


def accumulate(values, row_local, col_local, source, range_blocks, group_size):
    slot_count = values.shape[0]
    tile_size = values.shape[1]
    source_count = source.shape[0]
    feat_width = source.shape[2]
    flat_source = source.reshape(source_count, tile_size * feat_width)
    turn_count = slot_count // group_size
    source_ids = lax.broadcasted_iota(jnp.int32, (1, source_count), 1)
    block_ids = lax.broadcasted_iota(jnp.int32, (range_blocks, 1), 0)

    def one_turn(running, pieces):
        tile_vals, row_ids, col_ids = pieces
        col_hot = (col_ids[:, None] == source_ids).astype(jnp.bfloat16)
        picked = jnp.dot(col_hot, flat_source, preferred_element_type=jnp.float32).astype(
            jnp.bfloat16
        )
        picked = picked.reshape(group_size, tile_size, feat_width)
        products = jnp.einsum("sab,sbf->saf", tile_vals, picked, preferred_element_type=jnp.float32)
        row_hot = (block_ids == row_ids[None, :]).astype(jnp.float32)
        added = jnp.dot(
            row_hot,
            products.reshape(group_size, tile_size * feat_width),
            precision=lax.Precision.HIGHEST,
            preferred_element_type=jnp.float32,
        )
        return (running + added, None)

    start_sum = jnp.zeros((range_blocks, tile_size * feat_width), jnp.float32)
    running, _ = lax.scan(
        one_turn,
        start_sum,
        (
            values.reshape(turn_count, group_size, tile_size, tile_size),
            row_local.reshape(turn_count, group_size),
            col_local.reshape(turn_count, group_size),
        ),
    )
    return running.reshape(range_blocks * tile_size, feat_width)


def on_device(features, tile_values, tile_row, tile_col, weight_one, bias_one, weight_two):
    tile_size = tile_values.shape[1]
    dev_blocks = features.shape[0] // tile_size
    ba_count = lax.axis_size("ba")
    range_blocks = dev_blocks * ba_count
    row_local = local_rows(tile_row, range_blocks)
    col_local = local_columns(tile_col, dev_blocks, ba_count)
    gathered = lax.all_gather(features, "aa", axis=0, tiled=True)
    feature_blocks = gathered.reshape(-1, tile_size, gathered.shape[1])
    partial_value = accumulate(
        tile_values, row_local, col_local, feature_blocks, range_blocks, tile_values.shape[0]
    )
    summed = lax.psum(partial_value, "ba")
    own_rows = lax.dynamic_slice_in_dim(
        summed, lax.axis_index("ba") * dev_blocks * tile_size, dev_blocks * tile_size, 0
    )
    aggregated = own_rows.astype(jnp.bfloat16)
    hidden = jax.nn.relu(
        jnp.dot(aggregated, weight_one, preferred_element_type=jnp.float32) + bias_one
    ).astype(jnp.bfloat16)
    projected = jnp.dot(hidden, weight_two, preferred_element_type=jnp.float32).astype(jnp.bfloat16)
    gathered_rows = lax.all_gather(projected, "aa", axis=0, tiled=True)
    source_blocks = gathered_rows.reshape(-1, tile_size, projected.shape[1])
    slot_count = tile_values.shape[0]
    group_size = 16
    partial_out = accumulate(
        tile_values, row_local, col_local, source_blocks, range_blocks, group_size
    )
    result = lax.psum_scatter(partial_out, "ba", scatter_dimension=1, tiled=True)
    return result.astype(jnp.bfloat16)


def solution(mesh):
    return jax.shard_map(
        on_device,
        mesh=mesh,
        in_specs=(
            P(("aa", "ba"), None),
            P(("aa", "ba"), None, None),
            P(("aa", "ba")),
            P(("aa", "ba")),
            P(),
            P(),
            P(),
        ),
        out_specs=P("aa", "ba"),
        check_vma=False,
    )
```

profile of v0, /device:TPU:0, one launch (start us, length us, event | category | flops | bytes accessed | tf_op | source)
XLA Modules:
  0.0 797.6 jit_solution(8134527960323151522)
XLA Ops:
  6.5 0.7 all-gather.3.cloned.1.call-update
  7.3 0.0 all-gather.5.cloned.1.call-start
  7.3 0.7 compare_select_fusion
  8.0 0.7 fusion.18
  8.6 51.1 %all-gather.3.cloned.1.call-done = bf16[8192,128]{1,0:T(8,128)(2,1)} async-done(((bf16[512,128]{1,0:T(8,128)(2,1)}), bf16[8192,128]{1,0:T(8,128)(2,1)}) %all-gather.3.cloned.1.call-update) | async-done | bytes 2097168 | tf_op jit(solution)/shard_map/all_gather | solution.py:63
  59.8 4.2 reshape_reshape.6
  63.9 2.9 fusion.12
  66.8 1.2 copy.14
  68.1 0.9 copy-done.2
  69.0 6.3 convolution_bitcast_fusion
  75.3 9.4 %copy.10 = f32[128,128,128]{0,2,1:T(8,128)} copy(f32[128,128,128]{1,2,0:T(8,128)} %convolution_bitcast_fusion) | data formatting | bytes 16777216 | tf_op jit(solution)/shard_map/while/body/eval_jaxpr/sab,sbf->saf/dot_general | solution.py:33
  84.7 9.4 %fusion.16 = f32[32,16384]{1,0:T(8,128)} fusion(f32[128,16384]{0,1:T(8,128)} %bitcast.49, s32[128]{0:T(128)S(1)} %compare_select_fusion), kind=kOutput, calls=%fused_computation.27 | convolution fusion | flops 805310464 | bytes 10486272 | tf_op jit(solution)/shard_map/while/body/eval_jaxpr/dot_general | solution.py:35
  94.1 2.8 reshape.48
  96.9 73.9 %all-reduce.1 = bf16[4096,128]{1,0:T(8,128)(2,1)S(1)} all-reduce(f32[4096,128]{1,0:T(8,128)} %reshape.48), channel_id=1, replica_groups=mesh['aa'=16,'ba'=8] {'ba'}, use_global_device_ids=true, to_apply=%region_0.1 | all-reduce | flops 524288 | bytes 3145728 | tf_op jit(solution)/shard_map/psum | solution.py:68
  170.8 2.5 convolution_convert_fusion.2
  173.3 0.0 reduce-scatter.2.cloned.1.call-start
  173.4 0.1 reshape.45
  173.4 0.1 reshape.43
  173.5 106.3 %all-gather.5.cloned.1.call-done = bf16[8192,1024]{1,0:T(8,128)(2,1)} async-done(((bf16[512,1024]{1,0:T(8,128)(2,1)}), bf16[8192,1024]{1,0:T(8,128)(2,1)}) %all-gather.5.cloned.1.call-update) | async-done | bytes 16777232 | tf_op jit(solution)/shard_map/all_gather | solution.py:77
  279.9 17.0 %reshape_reshape.7 = bf16[64,131072]{1,0:T(8,128)(2,1)} reshape(bf16[8192,1024]{1,0:T(8,128)(2,1)} %all-gather.5.cloned.1.call-done) | data formatting | bytes 33554432 | tf_op jit(solution)/shard_map/reshape;reshape | solution.py:21
  296.8 310.0 %while.3 = (s32[]{:T(128)}, f32[32,131072]{1,0:T(8,128)}, s32[8,16]{1,0:T(8,128)S(1)}, bf16[8,16,128,128]{3,2,1,0:T(8,128)(2,1)}, s32[8,16]{1,0:T(8,128)S(1)}, /...) while((s32[]{:T(128)}, f32[32,131072]{1,0:T(8,128)}, s32[8,16]{1,0:T(8,128)S(1)}, ...), condition=%wide.region_2.3_spmd.clone, body=%wide.region_1.2_spmd.clone.sunk | while | flops 1621100032 | bytes 101188072 | solution.py:44
  296.8 8.1 %convolution_convert_fusion.4 = bf16[16,131072]{1,0:T(8,128)(2,1)S(1)} fusion(bf16[64,131072]{1,0:T(8,128)(2,1)} %get-tuple-element.173, s32[16]{0:T(128)S(1)} %get-tuple-element.150), kind=kOutput, calls=%fused_computation.3.clone.1 | convolution fusion | flops 270533632 | bytes 20971584 | tf_op jit(solution)/shard_map/while/body/eval_jaxpr/dot_general | solution.py:29
  305.0 2.3 copy.17
  307.3 2.3 fusion.43
  309.6 8.1 %copy.18 = f32[2,8,128,1024]{3,1,2,0:T(8,128)} copy(f32[2,8,128,1024]{3,2,1,0:T(8,128)S(1)} %bitcast.45) | data formatting | bytes 16777216 | tf_op jit(solution)/shard_map/while
  317.7 15.8 %convolution_add_fusion.2 = f32[32,131072]{1,0:T(8,128)} fusion(f32[16,131072]{1,0:T(8,128)} %bitcast.46, f32[32,131072]{1,0:T(8,128)} %get-tuple-element.161, pred[]{:T(512)S(6)} %compare.7, s32[16]{0:T(128)S(1)} %get-tuple-element.151), kind=kOutput, calls=%fused_computation.2.clone.1 | convolution fusion | flops 813695488 | bytes 41943104 | tf_op jit(solution)/shard_map/while/body/eval_jaxpr/dot_general | solution.py:35
  333.5 8.1 %convolution_convert_fusion.4 = bf16[16,131072]{1,0:T(8,128)(2,1)S(1)} fusion(bf16[64,131072]{1,0:T(8,128)(2,1)} %get-tuple-element.173, s32[16]{0:T(128)S(1)} %get-tuple-element.150), kind=kOutput, calls=%fused_computation.3.clone.1 | convolution fusion | flops 270533632 | bytes 20971584 | tf_op jit(solution)/shard_map/while/body/eval_jaxpr/dot_general | solution.py:29
  341.6 2.3 copy.17
  344.0 2.3 fusion.43
  346.3 8.1 %copy.18 = f32[2,8,128,1024]{3,1,2,0:T(8,128)} copy(f32[2,8,128,1024]{3,2,1,0:T(8,128)S(1)} %bitcast.45) | data formatting | bytes 16777216 | tf_op jit(solution)/shard_map/while
  354.3 18.2 %convolution_add_fusion.2 = f32[32,131072]{1,0:T(8,128)} fusion(f32[16,131072]{1,0:T(8,128)} %bitcast.46, f32[32,131072]{1,0:T(8,128)} %get-tuple-element.161, pred[]{:T(512)S(6)} %compare.7, s32[16]{0:T(128)S(1)} %get-tuple-element.151), kind=kOutput, calls=%fused_computation.2.clone.1 | convolution fusion | flops 813695488 | bytes 41943104 | tf_op jit(solution)/shard_map/while/body/eval_jaxpr/dot_general | solution.py:35
  372.6 8.1 %convolution_convert_fusion.4 = bf16[16,131072]{1,0:T(8,128)(2,1)S(1)} fusion(bf16[64,131072]{1,0:T(8,128)(2,1)} %get-tuple-element.173, s32[16]{0:T(128)S(1)} %get-tuple-element.150), kind=kOutput, calls=%fused_computation.3.clone.1 | convolution fusion | flops 270533632 | bytes 20971584 | tf_op jit(solution)/shard_map/while/body/eval_jaxpr/dot_general | solution.py:29
  380.7 2.3 copy.17
  383.0 2.3 fusion.43
  385.3 8.1 %copy.18 = f32[2,8,128,1024]{3,1,2,0:T(8,128)} copy(f32[2,8,128,1024]{3,2,1,0:T(8,128)S(1)} %bitcast.45) | data formatting | bytes 16777216 | tf_op jit(solution)/shard_map/while
  393.4 18.2 %convolution_add_fusion.2 = f32[32,131072]{1,0:T(8,128)} fusion(f32[16,131072]{1,0:T(8,128)} %bitcast.46, f32[32,131072]{1,0:T(8,128)} %get-tuple-element.161, pred[]{:T(512)S(6)} %compare.7, s32[16]{0:T(128)S(1)} %get-tuple-element.151), kind=kOutput, calls=%fused_computation.2.clone.1 | convolution fusion | flops 813695488 | bytes 41943104 | tf_op jit(solution)/shard_map/while/body/eval_jaxpr/dot_general | solution.py:35
  411.6 8.1 %convolution_convert_fusion.4 = bf16[16,131072]{1,0:T(8,128)(2,1)S(1)} fusion(bf16[64,131072]{1,0:T(8,128)(2,1)} %get-tuple-element.173, s32[16]{0:T(128)S(1)} %get-tuple-element.150), kind=kOutput, calls=%fused_computation.3.clone.1 | convolution fusion | flops 270533632 | bytes 20971584 | tf_op jit(solution)/shard_map/while/body/eval_jaxpr/dot_general | solution.py:29
  419.7 2.3 copy.17
  422.1 2.3 fusion.43
  424.4 8.1 %copy.18 = f32[2,8,128,1024]{3,1,2,0:T(8,128)} copy(f32[2,8,128,1024]{3,2,1,0:T(8,128)S(1)} %bitcast.45) | data formatting | bytes 16777216 | tf_op jit(solution)/shard_map/while
  432.4 18.2 %convolution_add_fusion.2 = f32[32,131072]{1,0:T(8,128)} fusion(f32[16,131072]{1,0:T(8,128)} %bitcast.46, f32[32,131072]{1,0:T(8,128)} %get-tuple-element.161, pred[]{:T(512)S(6)} %compare.7, s32[16]{0:T(128)S(1)} %get-tuple-element.151), kind=kOutput, calls=%fused_computation.2.clone.1 | convolution fusion | flops 813695488 | bytes 41943104 | tf_op jit(solution)/shard_map/while/body/eval_jaxpr/dot_general | solution.py:35
  450.7 8.1 %convolution_convert_fusion.4 = bf16[16,131072]{1,0:T(8,128)(2,1)S(1)} fusion(bf16[64,131072]{1,0:T(8,128)(2,1)} %get-tuple-element.173, s32[16]{0:T(128)S(1)} %get-tuple-element.150), kind=kOutput, calls=%fused_computation.3.clone.1 | convolution fusion | flops 270533632 | bytes 20971584 | tf_op jit(solution)/shard_map/while/body/eval_jaxpr/dot_general | solution.py:29
  458.8 2.3 copy.17
  461.1 2.3 fusion.43
  463.4 8.1 %copy.18 = f32[2,8,128,1024]{3,1,2,0:T(8,128)} copy(f32[2,8,128,1024]{3,2,1,0:T(8,128)S(1)} %bitcast.45) | data formatting | bytes 16777216 | tf_op jit(solution)/shard_map/while
  471.5 18.2 %convolution_add_fusion.2 = f32[32,131072]{1,0:T(8,128)} fusion(f32[16,131072]{1,0:T(8,128)} %bitcast.46, f32[32,131072]{1,0:T(8,128)} %get-tuple-element.161, pred[]{:T(512)S(6)} %compare.7, s32[16]{0:T(128)S(1)} %get-tuple-element.151), kind=kOutput, calls=%fused_computation.2.clone.1 | convolution fusion | flops 813695488 | bytes 41943104 | tf_op jit(solution)/shard_map/while/body/eval_jaxpr/dot_general | solution.py:35
  489.7 8.1 %convolution_convert_fusion.4 = bf16[16,131072]{1,0:T(8,128)(2,1)S(1)} fusion(bf16[64,131072]{1,0:T(8,128)(2,1)} %get-tuple-element.173, s32[16]{0:T(128)S(1)} %get-tuple-element.150), kind=kOutput, calls=%fused_computation.3.clone.1 | convolution fusion | flops 270533632 | bytes 20971584 | tf_op jit(solution)/shard_map/while/body/eval_jaxpr/dot_general | solution.py:29
  497.8 2.3 copy.17
  500.1 2.3 fusion.43
  502.5 8.1 %copy.18 = f32[2,8,128,1024]{3,1,2,0:T(8,128)} copy(f32[2,8,128,1024]{3,2,1,0:T(8,128)S(1)} %bitcast.45) | data formatting | bytes 16777216 | tf_op jit(solution)/shard_map/while
  510.5 18.2 %convolution_add_fusion.2 = f32[32,131072]{1,0:T(8,128)} fusion(f32[16,131072]{1,0:T(8,128)} %bitcast.46, f32[32,131072]{1,0:T(8,128)} %get-tuple-element.161, pred[]{:T(512)S(6)} %compare.7, s32[16]{0:T(128)S(1)} %get-tuple-element.151), kind=kOutput, calls=%fused_computation.2.clone.1 | convolution fusion | flops 813695488 | bytes 41943104 | tf_op jit(solution)/shard_map/while/body/eval_jaxpr/dot_general | solution.py:35
  528.7 8.1 %convolution_convert_fusion.4 = bf16[16,131072]{1,0:T(8,128)(2,1)S(1)} fusion(bf16[64,131072]{1,0:T(8,128)(2,1)} %get-tuple-element.173, s32[16]{0:T(128)S(1)} %get-tuple-element.150), kind=kOutput, calls=%fused_computation.3.clone.1 | convolution fusion | flops 270533632 | bytes 20971584 | tf_op jit(solution)/shard_map/while/body/eval_jaxpr/dot_general | solution.py:29
  536.9 2.3 copy.17
  539.2 2.3 fusion.43
  541.5 8.1 %copy.18 = f32[2,8,128,1024]{3,1,2,0:T(8,128)} copy(f32[2,8,128,1024]{3,2,1,0:T(8,128)S(1)} %bitcast.45) | data formatting | bytes 16777216 | tf_op jit(solution)/shard_map/while
  549.6 18.2 %convolution_add_fusion.2 = f32[32,131072]{1,0:T(8,128)} fusion(f32[16,131072]{1,0:T(8,128)} %bitcast.46, f32[32,131072]{1,0:T(8,128)} %get-tuple-element.161, pred[]{:T(512)S(6)} %compare.7, s32[16]{0:T(128)S(1)} %get-tuple-element.151), kind=kOutput, calls=%fused_computation.2.clone.1 | convolution fusion | flops 813695488 | bytes 41943104 | tf_op jit(solution)/shard_map/while/body/eval_jaxpr/dot_general | solution.py:35
  567.8 8.1 %convolution_convert_fusion.4 = bf16[16,131072]{1,0:T(8,128)(2,1)S(1)} fusion(bf16[64,131072]{1,0:T(8,128)(2,1)} %get-tuple-element.173, s32[16]{0:T(128)S(1)} %get-tuple-element.150), kind=kOutput, calls=%fused_computation.3.clone.1 | convolution fusion | flops 270533632 | bytes 20971584 | tf_op jit(solution)/shard_map/while/body/eval_jaxpr/dot_general | solution.py:29
  575.9 2.3 copy.17
  578.2 2.3 fusion.43
  580.6 8.1 %copy.18 = f32[2,8,128,1024]{3,1,2,0:T(8,128)} copy(f32[2,8,128,1024]{3,2,1,0:T(8,128)S(1)} %bitcast.45) | data formatting | bytes 16777216 | tf_op jit(solution)/shard_map/while
  588.6 18.2 %convolution_add_fusion.2 = f32[32,131072]{1,0:T(8,128)} fusion(f32[16,131072]{1,0:T(8,128)} %bitcast.46, f32[32,131072]{1,0:T(8,128)} %get-tuple-element.161, pred[]{:T(512)S(6)} %compare.7, s32[16]{0:T(128)S(1)} %get-tuple-element.151), kind=kOutput, calls=%fused_computation.2.clone.1 | convolution fusion | flops 813695488 | bytes 41943104 | tf_op jit(solution)/shard_map/while/body/eval_jaxpr/dot_general | solution.py:35
  606.8 12.1 %reshape.49 = f32[4096,1024]{1,0:T(8,128)} reshape(f32[32,131072]{1,0:T(8,128)} %get-tuple-element.71) | data formatting | bytes 33554432 | tf_op jit(solution)/shard_map/reshape | solution.py:53
  619.0 169.4 %reduce-scatter.2.cloned.1.call-done = f32[4096,128]{1,0:T(8,128)} async-done(((f32[4096,1024]{1,0:T(8,128)}), f32[4096,128]{1,0:T(8,128)}) %reduce-scatter.2.cloned.1.call-update) | async-done | bytes 2097168 | tf_op jit(solution)/shard_map/reduce_scatter | solution.py:84
  788.4 2.7 convert_element_type.29
  (21 shorter events, 0.1 us)
Async XLA Ops:
  6.5 164.2 %copy-start = (bf16[1024,1024]{1,0:T(8,128)(2,1)S(1)}, bf16[1024,1024]{1,0:T(8,128)(2,1)}, u32[]{:S(2)}) copy-start(bf16[1024,1024]{1,0:T(8,128)(2,1)} %param.15) | copy-start | bytes 6291460
  6.5 53.2 %all-gather.3.cloned.1.call-start = ((), (), s32[]{:S(2)}) async-start(), calls=%async_computation.1 | async-start | bytes 2228224 | tf_op jit(solution)/shard_map/all_gather | solution.py:63
  7.3 272.6 %all-gather.5.cloned.1.call-start = ((), (), s32[]{:S(2)}) async-start(), calls=%async_computation.2 | async-start | bytes 17825792 | tf_op jit(solution)/shard_map/all_gather | solution.py:77
  66.8 2.2 copy-start.2
  94.1 76.7 %copy-start.3 = (bf16[128,1024]{1,0:T(8,128)(2,1)S(1)}, bf16[128,1024]{1,0:T(8,128)(2,1)}, u32[]{:S(2)}) copy-start(bf16[128,1024]{1,0:T(8,128)(2,1)} %param.13) | copy-start | bytes 786436
  94.1 76.7 %copy-start.4 = (f32[1024]{0:T(1024)S(1)}, f32[1024]{0:T(1024)}, u32[]{:S(2)}) copy-start(f32[1024]{0:T(1024)} %param.14) | copy-start | bytes 12292
  173.3 615.1 %reduce-scatter.2.cloned.1.call-start = ((), (), s32[]{:S(2)}) async-start(), calls=%async_computation.3 | async-start | bytes 18874368 | tf_op jit(solution)/shard_map/reduce_scatter | solution.py:84
  619.0 172.1 %copy-start.1 = (bf16[1024,1024]{1,0:T(8,128)(2,1)S(1)}, bf16[1024,1024]{1,0:T(8,128)(2,1)}, u32[]{:S(2)}) copy-start(bf16[1024,1024]{1,0:T(8,128)(2,1)} %param.15) | copy-start | bytes 6291460
Sparse Core Ops, SparseCore 0:
  9.8 49.8 all-gather.2
  173.4 106.3 all-gather.4
  619.1 169.2 reduce-scatter.1
where the time goes:
time: 800 us; the launch traced here: 798 us
  waiting for transfers between devices  328 us (41%)
  matrix products  248 us (31%)
  local copies, waits for them, and re-layouts  131 us (16%)
  blocking collectives  73.9 us (9%)
  between operations  13.2 us (2%)
    reduce_scatter x1, waiting for transfers between devices, on_device(): lax.psum_scatter(partial_out, 'ba', scatter_dimension=1, tiled=True)  169 us
    dot_general x9, matrix products, one_turn(): jnp.dot(row_hot, products.reshape(group_size, tile_size * feat_width), pr...  153 us
    all_gather x1, waiting for transfers between devices, on_device(): gathered_rows = lax.all_gather(projected, 'aa', axis=0, tiled=True)  106 us
    while x16, local copies, waits for them, and re-layouts  83.1 us
    psum x1, blocking collectives, on_device(): summed = lax.psum(partial_value, 'ba')  73.9 us
    dot_general x9, matrix products, one_turn(): jnp.dot(col_hot, flat_source, preferred_element_type=jnp.float32)  67.7 us
    all_gather x1, waiting for transfers between devices, on_device(): gathered = lax.all_gather(features, 'aa', axis=0, tiled=True)  51.1 us
    dot_general x9, matrix products, one_turn(): jnp.einsum('sab,sbf->saf', tile_vals, picked, preferred_element_type=jnp....  24.7 us
  transfers between devices with their start and end apart: 3, of which 3 were waited for; matrix products, arithmetic and copies ran while one was open for 0% of the time, Pallas kernels for 0%

commit v1 on v0

v1 whole, which is shorter than its diff:
```python
import functools

import jax
import jax.numpy as jnp
from jax import lax
from jax.experimental import pallas as pl
from jax.experimental.pallas import tpu as pltpu
from jax.sharding import PartitionSpec as P

MESH = pl.DeviceIdType.MESH
TILE = 128
NZ = 4
NB = 8
NA = 16
RB = 32
N1 = 18
H1 = N1 // 2
N2 = RB - N1
H2 = N2 // 2
M0P, M0M, M1P, M1M, M2P, M2M = 0, N1, 2 * N1, 3 * N1, 4 * N1, 5 * N1
XS = 6 * N1
T2 = XS + 4 * N2
T1 = T2 + N2
T3 = T1 + N2
XF = T3 + N2
BLOCKS = XF + N1
PAIRS = 80
BF = jnp.bfloat16
F32 = jnp.float32
CT = jnp.float32


def prepare(tile_row, tile_col):
    slots = tile_row.shape[0]
    row = jnp.where(tile_row < 0, -1, tile_row % RB)
    clamped = jnp.maximum(tile_col, 0)
    col = clamped // (4 * NB) * 4 + clamped % 4
    blocks = jnp.arange(RB, dtype=jnp.int32)
    ids = jnp.arange(slots, dtype=jnp.int32)
    hot = row[:, None] == blocks[None, :]
    count = jnp.sum(hot, axis=0, dtype=jnp.int32)
    pairs = (count + 1) // 2
    start = jnp.sum(jnp.where(blocks[None, :] < blocks[:, None], pairs[None, :], 0), axis=1)
    rank = jnp.sum((row[:, None] == row[None, :]) & (ids[None, :] < ids[:, None]), axis=1, dtype=jnp.int32)
    place = jnp.where(row >= 0, 2 * jnp.sum(jnp.where(hot, start[None, :], 0), axis=1) + rank, -1)
    positions = jnp.arange(2 * PAIRS, dtype=jnp.int32)
    match = place[None, :] == positions[:, None]
    slot_at = slots + jnp.sum(jnp.where(match, ids[None, :] - slots, 0), axis=1)
    col_at = jnp.sum(jnp.where(match, col[None, :], 0), axis=1)
    q = jnp.arange(PAIRS, dtype=jnp.int32)
    inside = (q[:, None] > start[None, :]) & (q[:, None] < (start + pairs)[None, :])
    keep = jnp.sum(inside, axis=1).astype(F32)
    last = jnp.where(count > 0, start + pairs - 1, PAIRS)
    return slot_at, col_at, keep, last


def kernel(
    slot_at, col_at, keep, last, x_ref, tiles_hbm, w1_ref, b1_ref, w2_hbm, out_ref,
    tiles, w2c, feats, send_c, recv_c, lows, sb, rb,
    loc_sem, as_sem, ar_sem, fs_sem, fr_sem, cs_sem, cr_sem, ds_sem, dr_sem, gs_sem, gr_sem, es_sem, er_sem,
):
    a, b = lax.axis_index("aa"), lax.axis_index("ba")
    y, xh, c = a // 4, lax.rem(a // 2, 2), lax.rem(a, 2)
    xl, z = b // NZ, lax.rem(b, NZ)

    def aa_of(dy, dx):
        return lax.rem(y + dy, 4) * 4 + lax.rem(xh + dx, 2) * 2 + c

    def ba_of(dx, dz):
        return lax.rem(xl + dx, 2) * NZ + lax.rem(z + dz, NZ)

    sibling = (a + 1 - 2 * c, b)

    tile_copy = pltpu.make_async_copy(tiles_hbm, tiles.at[pl.ds(0, 128)], loc_sem.at[0])
    tile_copy.start()
    w2_copies = []
    for f in range(NB):
        w2_copies.append(
            pltpu.make_async_copy(
                w2_hbm.at[:, pl.ds(f * TILE, TILE)],
                w2c.at[f],
                loc_sem.at[1 + f],
            )
        )
        w2_copies[-1].start()

    barrier = pltpu.get_barrier_semaphore()
    for k in range(1, 8):
        pl.semaphore_signal(barrier, inc=1, device_id=(aa_of(k // 2, k % 2), b), device_id_type=MESH)
        pl.semaphore_signal(barrier, inc=1, device_id=(a, ba_of(k // NZ, k % NZ)), device_id_type=MESH)
    pl.semaphore_signal(barrier, inc=1, device_id=sibling, device_id_type=MESH)

    tiles[128] = jnp.zeros((TILE, TILE), BF)
    feats[pl.ds(a * 4, 4)] = x_ref[...].reshape(4, TILE, TILE)

    pl.semaphore_wait(barrier, 15)

    def gather(buf, s_sem, r_sem, s_fwd, r_fwd, use):
        def block(owner):
            return buf.at[pl.ds(owner * 4, 4)]

        def to_peer(k):
            peer = aa_of(k // 2, lax.rem(k, 2))
            return pltpu.make_async_remote_copy(
                src_ref=block(a), dst_ref=block(a), send_sem=s_sem.at[k], recv_sem=r_sem.at[k],
                device_id=(peer, b), device_id_type=MESH,
            )

        def forward(k):
            owner = aa_of(4 - k // 2, lax.rem(k, 2))
            return pltpu.make_async_remote_copy(
                src_ref=block(owner), dst_ref=block(owner), send_sem=s_fwd.at[k], recv_sem=r_fwd.at[k],
                device_id=sibling, device_id_type=MESH,
            )

        def start(i, carry):
            to_peer(8 - i).start()
            return carry

        lax.fori_loop(1, 8, start, 0)
        forward(0).start()
        if use is not None:
            use(a)
            forward(0).wait_recv()
            use(a + 1 - 2 * c)

        def pass_on(k, carry):
            to_peer(k).wait_recv()
            forward(k).start()
            if use is not None:
                use(aa_of(4 - k // 2, lax.rem(k, 2)))
            return carry

        lax.fori_loop(1, 8, pass_on, 0)

        def take(k, carry):
            forward(k).wait_recv()
            if use is not None:
                use(aa_of(4 - k // 2, lax.rem(k, 2)) + 1 - 2 * c)
            return carry

        lax.fori_loop(0 if use is None else 1, 8, take, 0)

        def finish():
            def body(k, carry):
                to_peer(k).wait_send()
                forward(k).wait_send()
                return carry

            lax.fori_loop(1, 8, body, 0)
            forward(0).wait_send()

        return finish

    finish_a = gather(feats, as_sem, ar_sem, fs_sem, fr_sem, None)
    tile_copy.wait()

    group = 4

    def pair_products(source, width, acc, store):
        acc[:, pl.ds(0, width)] = jnp.zeros((TILE, width), F32)

        def body(i, carry):
            running = acc[:, pl.ds(0, width)]
            for j in range(group):
                q = i * group + j
                left = jnp.concatenate([tiles[slot_at[2 * q]], tiles[slot_at[2 * q + 1]]], axis=1)
                right = jnp.concatenate([source[col_at[2 * q]], source[col_at[2 * q + 1]]], axis=0)
                running = running * keep[q] + jnp.dot(left, right, preferred_element_type=F32)
                store(q, running)
            acc[:, pl.ds(0, width)] = running
            return carry

        lax.fori_loop(0, PAIRS // group, body, 0)

    def each(count, body):
        def one(i, carry):
            body(i)
            return carry

        lax.fori_loop(0, count, one, 0)

    def layer_one(sums1, acc):
        sums1[PAIRS] = jnp.zeros((TILE, TILE), F32)

        def store1(q, value):
            sums1[q] = value

        pair_products(feats, TILE, acc, store1)

        def pick1(r):
            send_c[r] = sums1[last[r]].astype(send_c.dtype)

        each(RB, pick1)

    pl.run_scoped(layer_one, pltpu.VMEM((PAIRS + 1, TILE, TILE), F32), pltpu.VMEM((TILE, TILE), F32))

    def exchange_c(k):
        peer = ba_of(k // NZ, k % NZ)
        return pltpu.make_async_remote_copy(
            src_ref=send_c.at[pl.ds(peer * 4, 4)], dst_ref=recv_c.at[k - 1], send_sem=cs_sem.at[k], recv_sem=cr_sem.at[k],
            device_id=(a, peer), device_id_type=MESH,
        )

    for k in (6, 2, 5, 7, 1, 3, 4):
        exchange_c(k).start()
    total = send_c[pl.ds(b * 4, 4)].astype(F32)
    for k in (4, 1, 3, 5, 7, 2, 6):
        exchange_c(k).wait_recv()
        total = total + recv_c[k - 1].astype(F32)
    lows[pl.ds(a * 4, 4)] = total.astype(BF)
    for k in range(1, 8):
        exchange_c(k).wait_send()
    finish_a()

    zp, zm = (a, ba_of(0, 1)), (a, ba_of(0, 3))
    xn = (a, ba_of(1, 0))

    def message(i, offset, count, peer):
        return pltpu.make_async_remote_copy(
            src_ref=sb.at[pl.ds(offset, count)], dst_ref=rb.at[pl.ds(offset, count)],
            send_sem=es_sem.at[i], recv_sem=er_sem.at[i], device_id=peer, device_id_type=MESH,
        )

    m0p, m0m = message(0, M0P, N1, zp), message(1, M0M, N1, zm)
    xs2 = message(2, XS + 2 * N2, N2, xn)
    m1pb, m1ma = message(3, M1P + H1, H1, zp), message(4, M1M, H1, zm)
    xs1, xs3 = message(5, XS + N2, N2, xn), message(6, XS + 3 * N2, N2, xn)
    t2p, t2m = message(7, T2, H2, zp), message(8, T2 + H2, H2, zm)
    m1pa, m1mb = message(9, M1P, H1, zp), message(10, M1M + H1, H1, zm)
    m2p, m2m = message(11, M2P, N1, zp), message(12, M2M, N1, zm)
    t1b, t3a = message(13, T1 + H2, H2, zp), message(14, T3, H2, zm)
    t1a, t3b = message(15, T1, H2, zp), message(16, T3 + H2, H2, zm)
    xs0 = message(17, XS, N2, xn)
    xfa, xfb = message(18, XF, H1, xn), message(19, XF + H1, H1, xn)
    messages = [m0p, m0m, xs2, m1pb, m1ma, xs1, xs3, t2p, t2m, m1pa, m1mb, m2p, m2m, t1b, t3a, t1a, t3b, xs0, xfa, xfb]

    def layer_two(hid, proj_a, proj_b, sums2, acc):
        sums2[PAIRS] = jnp.zeros((TILE, 2 * TILE), BF)

        def columns(pair):
            (dx0, dz0), (dx1, dz1) = pair
            return jnp.concatenate([w2c[ba_of(dx0, dz0)], w2c[ba_of(dx1, dz1)]], axis=1)

        steps = (((0, 2), (1, 2)), ((1, 1), (1, 3)), ((0, 1), (0, 3)), ((0, 0), (1, 0)))

        def project(owner, s, proj):
            value = jnp.dot(hid[owner], columns(steps[s]), preferred_element_type=F32)
            proj[pl.ds(owner * 4, 4)] = value.astype(BF).reshape(4, TILE, 2 * TILE)

        def hidden_of(owner):
            rows = lows[pl.ds(owner * 4, 4)].reshape(4 * TILE, TILE)
            value = jnp.dot(rows, w1_ref[...], preferred_element_type=F32) + b1_ref[...]
            hid[owner] = jnp.maximum(value, 0.0).astype(BF)
            project(owner, 0, proj_a)
            project(owner, 1, proj_b)

        finish_d = gather(lows, ds_sem, dr_sem, gs_sem, gr_sem, hidden_of)
        finish_d()

        def store2(q, value):
            sums2[q] = value.astype(BF)

        def pick(r):
            value = sums2[last[r]].astype(F32)
            return value[:, :TILE], value[:, TILE:]

        def got(i):
            return rb[i].astype(F32)

        def put(i, value):
            sb[i] = value.astype(BF)

        pair_products(proj_a, 2 * TILE, acc, store2)

        def body(i):
            near, far = pick(i)
            put(M0P + i, near)
            put(M0P + H1 + i, far)
            near, far = pick(H1 + i)
            put(M0M + i, near)
            put(M0M + H1 + i, far)

        each(H1, body)
        m0p.start()
        m0m.start()

        def body(i):
            near, far = pick(N1 + i)
            put(T2 + i, near)
            put(XS + 2 * N2 + i, far)

        each(N2, body)
        xs2.start()

        pair_products(proj_b, 2 * TILE, acc, store2)

        def body(i):
            plus, minus = pick(N1 + i)
            put(XS + N2 + i, plus)
            put(XS + 3 * N2 + i, minus)

        each(N2, body)
        xs1.start()
        xs3.start()

        def body(i):
            put(M1M + i, pick(i)[1])
            put(M1P + H1 + i, pick(H1 + i)[0])

        each(H1, body)
        m1pb.start()
        m1ma.start()

        each(NA, lambda owner: project(owner, 2, proj_a))
        m0p.wait_recv()
        m0m.wait_recv()

        def body(i):
            put(M1P + i, pick(i)[0] + got(M0P + H1 + i))
            put(M1M + H1 + i, pick(H1 + i)[1] + got(M0M + H1 + i))

        each(H1, body)
        m1pa.start()
        m1mb.start()
        xs2.wait_recv()

        def body(i):
            put(T2 + i, sb[T2 + i].astype(F32) + got(XS + 2 * N2 + i))

        each(N2, body)
        t2p.start()
        t2m.start()

        pair_products(proj_a, 2 * TILE, acc, store2)

        def body(i):
            plus, minus = pick(i)
            put(M2P + i, plus + got(M0P + i))
            put(M2M + i, minus)
            plus, minus = pick(H1 + i)
            put(M2P + H1 + i, plus)
            put(M2M + H1 + i, minus + got(M0M + i))

        each(H1, body)
        m2p.start()
        m2m.start()
        xs1.wait_recv()
        xs3.wait_recv()

        def body(i):
            plus, minus = pick(N1 + i)
            put(T1 + i, plus + got(XS + N2 + i))
            put(T3 + i, minus + got(XS + 3 * N2 + i))

        each(N2, body)
        t1b.start()
        t3a.start()

        each(NA, lambda owner: project(owner, 3, proj_b))
        t2p.wait_recv()
        t2m.wait_recv()

        def body(i):
            put(T1 + i, sb[T1 + i].astype(F32) + got(T2 + i))
            put(T3 + H2 + i, sb[T3 + H2 + i].astype(F32) + got(T2 + H2 + i))

        each(H2, body)
        t1a.start()
        t3b.start()

        pair_products(proj_b, 2 * TILE, acc, store2)

        def body(i):
            put(XS + i, pick(N1 + i)[1])

        each(N2, body)
        xs0.start()
        m1pb.wait_recv()
        m1ma.wait_recv()
        m1pa.wait_recv()
        m1mb.wait_recv()

        def body(i):
            put(XF + i, pick(i)[1] + got(M1P + i) + got(M1M + i))

        each(H1, body)
        xfa.start()

        def body(i):
            j = H1 + i
            put(XF + j, pick(j)[1] + got(M1P + j) + got(M1M + j))

        each(H1, body)
        xfb.start()

        def write(r, value):
            out_ref[pl.ds(pl.multiple_of(r * TILE, TILE), TILE), :] = value.astype(BF)

        xs0.wait_recv()
        t1b.wait_recv()
        t1a.wait_recv()
        t3a.wait_recv()
        t3b.wait_recv()

        def body(i):
            write(N1 + i, pick(N1 + i)[0] + got(XS + i) + got(T1 + i) + got(T3 + i))

        each(N2, body)
        m2p.wait_recv()
        m2m.wait_recv()
        for start, copy in ((0, xfa), (H1, xfb)):
            copy.wait_recv()

            def body(i):
                j = start + i
                write(j, pick(j)[0] + got(M2P + j) + got(M2M + j) + got(XF + j))

            each(H1, body)
        for copy in messages:
            copy.wait_send()

    for copy in w2_copies:
        copy.wait()
    pl.run_scoped(
        layer_two,
        pltpu.VMEM((NA, 4 * TILE, 1024), BF),
        pltpu.VMEM((64, TILE, 2 * TILE), BF),
        pltpu.VMEM((64, TILE, 2 * TILE), BF),
        pltpu.VMEM((PAIRS + 1, TILE, 2 * TILE), BF),
        pltpu.VMEM((TILE, 2 * TILE), F32),
    )


def on_device(features, tile_values, tile_row, tile_col, weight_one, bias_one, weight_two):
    slot_at, col_at, keep, last = prepare(tile_row, tile_col)
    smem = pl.BlockSpec(memory_space=pltpu.SMEM)
    vmem = pl.BlockSpec(memory_space=pltpu.VMEM)
    hbm = pl.BlockSpec(memory_space=pl.ANY)
    dma = pltpu.SemaphoreType.DMA
    return pl.pallas_call(
        kernel,
        out_shape=jax.ShapeDtypeStruct((RB * TILE, TILE), BF),
        in_specs=[smem, smem, smem, smem, vmem, hbm, vmem, vmem, hbm],
        out_specs=vmem,
        scratch_shapes=[
            pltpu.VMEM((129, TILE, TILE), BF),
            pltpu.VMEM((NB, 1024, TILE), BF),
            pltpu.VMEM((64, TILE, TILE), BF),
            pltpu.VMEM((RB, TILE, TILE), CT),
            pltpu.VMEM((7, 4, TILE, TILE), CT),
            pltpu.VMEM((64, TILE, TILE), BF),
            pltpu.VMEM((BLOCKS, TILE, TILE), BF),
            pltpu.VMEM((BLOCKS, TILE, TILE), BF),
        ]
        + [dma((9,))]
        + [dma((8,))] * 10
        + [dma((20,))] * 2,
        compiler_params=pltpu.CompilerParams(
            collective_id=0, has_side_effects=True, vmem_limit_bytes=64 * 2**20 - 2**16
        ),
        cost_estimate=pl.CostEstimate(flops=26 * 10**9, bytes_accessed=8 * 2**20, transcendentals=0),
        name="two_layers",
    )(slot_at, col_at, keep, last, features, tile_values, weight_one, bias_one.reshape(1, -1), weight_two)


def solution(mesh):
    return jax.shard_map(
        on_device,
        mesh=mesh,
        in_specs=(
            P(("aa", "ba"), None),
            P(("aa", "ba"), None, None),
            P(("aa", "ba")),
            P(("aa", "ba")),
            P(),
            P(),
            P(),
        ),
        out_specs=P("aa", "ba"),
        check_vma=False,
    )
```

time: 800 us -> 163 us (0.20)
  waiting for transfers between devices: 328 us -> 0 us
  matrix products: 248 us -> 0 us
  Pallas kernels: 0 us -> 156 us
  local copies, waits for them, and re-layouts: 131 us -> 2.26 us
  blocking collectives: 73.9 us -> 0 us
  between operations: 13.2 us -> 0.03 us
    dot_general x28 -> x0, matrix products: 248 us -> none  [the longest x9 153 us: one_turn(): jnp.dot(row_hot, products.reshape(group_size, tile_size * feat_width), pr...]
    reduce_scatter x1 -> x0, waiting for transfers between devices: 169 us -> none  [on_device(): lax.psum_scatter(partial_out, 'ba', scatter_dimension=1, tiled=True)]
    all_gather x2 -> x0, waiting for transfers between devices: 157 us -> none  [the longest x1 106 us: on_device(): gathered_rows = lax.all_gather(projected, 'aa', axis=0, tiled=True)]
    pallas_call x0 -> x1, Pallas kernels: none -> 156 us  [on_device(): pl.pallas_call(kernel, out_shape=jax.ShapeDtypeStruct((RB * TILE, TILE),...]
    while x16 -> x0, local copies, waits for them, and re-layouts: 83.1 us -> none
    psum x1 -> x0, blocking collectives: 73.9 us -> none  [on_device(): summed = lax.psum(partial_value, 'ba')]
    another operation x2 -> x0, local copies, waits for them, and re-layouts: 21.1 us -> none  [accumulate(): flat_source = source.reshape(source_count, tile_size * feat_width)]
    reshape x4 -> x0, local copies, waits for them, and re-layouts: 15 us -> none  [the longest x2 14.9 us: accumulate(): return running.reshape(range_blocks * tile_size, feat_width)]
  transfers between devices with their start and end apart: 3 -> 0, of which waited for: 3 -> 0; matrix products, arithmetic and copies ran while one was open for 0% -> 0% of each run, Pallas kernels for 0% -> 0%
where the time goes in v1:
time: 163 us
  Pallas kernels  156 us (96%)
  other arithmetic  4.29 us (3%)
  local copies, waits for them, and re-layouts  2.26 us (1%)
    pallas_call x1, Pallas kernels, on_device(): pl.pallas_call(kernel, out_shape=jax.ShapeDtypeStruct((RB * TILE, TILE),...  156 us

profile of v1, /device:TPU:0, one launch (start us, length us, event | category | flops | bytes accessed | tf_op | source)
XLA Modules:
  0.0 162.9 jit_solution(3471968302559388211)
XLA Ops:
  0.0 0.7 compare_select_fusion.5
  0.7 0.1 convert_reduce_fusion.2
  0.8 0.1 select_reduce_fusion.3
  0.9 0.1 select_reduce_fusion.2
  1.0 0.2 convert_reduce_fusion
  1.2 0.7 compare_select_fusion.1
  1.9 0.7 select_reduce_fusion
  2.6 0.5 compare_select_fusion
  3.1 0.1 convert_reduce_fusion.1
  3.2 0.5 convert_element_type.15.keep
  3.7 0.6 broadcast_add_fusion.slot_at
  4.3 156.3 %two_layers.1 = bf16[4096,128]{1,0:T(8,128)(2,1)} custom-call(s32[160]{0:T(256)} %broadcast_add_fusion.slot_at, s32[160]{0:T(256)} %get-tuple-element.5.col_at, f32[80]{0:T(128)} %convert_element_type.15.keep, s32[32]{0:T(128)} %get-tuple-element.7.last, bf16[512,128]{1,0:T(8,128)(2,1)} %x_ref.1, bf16[128,128,128]{2,1,0:T(8,128)(2,1)} %tiles_hbm.1, ...), custom_call_target="tpu_custom_call" | custom-call | flops 25999998976 | bytes 8388608 | tf_op jit(solution)/shard_map/two_layers/pallas_call | solution.py:441
  160.6 2.3 %copy.9 = bf16[4096,128]{1,0:T(8,128)(2,1)} copy(bf16[4096,128]{1,0:T(8,128)(2,1)} %two_layers.1) | data formatting | bytes 2097152
  (2 shorter events, 0.0 us)

commit v2 on v1

v2 whole, which is shorter than its diff:
```python
import functools

import jax
import jax.numpy as jnp
from jax import lax
from jax.experimental import pallas as pl
from jax.experimental.pallas import tpu as pltpu
from jax.sharding import PartitionSpec as P

MESH = pl.DeviceIdType.MESH
TILE = 128
NZ = 4
NB = 8
NA = 16
RB = 32
N1 = 18
H1 = N1 // 2
N2 = RB - N1
H2 = N2 // 2
M0P, M0M, M1P, M1M, M2P, M2M = 0, N1, 2 * N1, 3 * N1, 4 * N1, 5 * N1
XS = 6 * N1
T2 = XS + 4 * N2
T1 = T2 + N2
T3 = T1 + N2
XF = T3 + N2
BLOCKS = XF + N1
PAIRS = 80
BF = jnp.bfloat16
F32 = jnp.float32
C_M0P, C_M0M, C_M1P, C_M1M, C_XS, C_T2, C_T1, C_T3, C_XF, C_BLOCKS = 0, 2, 4, 8, 12, 20, 22, 24, 26, 28


def prepare(tile_row, tile_col, index_v, keep_v):
    slots = TILE
    square = (slots, slots)

    def iota(dim, shape=square):
        return lax.broadcasted_iota(jnp.int32, shape, dim)

    def over_rows(x):
        return jnp.sum(x, axis=0, keepdims=True)

    def over_lanes(x):
        return jnp.sum(x, axis=1, keepdims=True)

    row_l = jnp.broadcast_to(jnp.where(tile_row < 0, -1, tile_row & (RB - 1)), square)
    clamped = jnp.maximum(tile_col, 0)
    col_l = jnp.broadcast_to((clamped >> 5) * 4 + (clamped & 3), square)
    row_s, col_s = row_l.T, col_l.T
    down, across = iota(0), iota(1)
    zero, one = jnp.zeros(square, jnp.int32), jnp.ones(square, jnp.int32)

    hot = row_s == across
    count_l = over_rows(jnp.where(hot, one, zero))
    count_s = over_lanes(jnp.where(row_l == down, one, zero))
    pairs_l, pairs_s = (count_l + 1) >> 1, (count_s + 1) >> 1
    start_l = over_rows(jnp.where(down < across, pairs_s, zero))
    start_s = over_lanes(jnp.where(across < down, pairs_l, zero))
    rank_s = over_lanes(jnp.where((row_l == row_s) & (across < down), one, zero))
    slot_start = over_lanes(jnp.where(hot, start_l, zero))
    place = jnp.where(row_s[:, :1] >= 0, 2 * slot_start + rank_s, -1)
    wide = (slots, 2 * TILE)
    match = place == iota(1, wide)
    nothing = jnp.zeros(wide, jnp.int32)
    slot_at = slots + over_rows(jnp.where(match, iota(0, wide) - slots, nothing))
    col_at = over_rows(jnp.where(match, col_s[:, :1], nothing))
    inside = (across > start_s) & (across < start_s + pairs_s)
    last = jnp.where(count_l > 0, start_l + pairs_l - 1, PAIRS)
    index_v[...] = jnp.zeros(index_v.shape, jnp.int32)
    index_v[0:1, :] = slot_at
    index_v[1:2, :] = col_at
    index_v[2:3, 0:TILE] = last
    keep_v[0:1, :] = over_rows(jnp.where(inside, one, zero)).astype(F32)


def kernel(
    row_ref, col_ref, x_ref, tiles_hbm, w1_ref, b1_ref, w2_hbm, out_ref,
    tiles, w2c, feats, cr, lows, sb, rb, index_v, keep_v, index, keeps,
    loc_sem, as_sem, ar_sem, fs_sem, fr_sem, cs_sem, cr_sem, ds_sem, dr_sem, gs_sem, gr_sem, es_sem, er_sem,
):
    a, b = lax.axis_index("aa"), lax.axis_index("ba")
    y, xh, c = a // 4, lax.rem(a // 2, 2), lax.rem(a, 2)
    xl, z = b // NZ, lax.rem(b, NZ)

    def aa_of(dy, dx):
        return lax.rem(y + dy, 4) * 4 + lax.rem(xh + dx, 2) * 2 + c

    def ba_of(dx, dz):
        return lax.rem(xl + dx, 2) * NZ + lax.rem(z + dz, NZ)

    sibling = (a + 1 - 2 * c, b)
    zp, zm = (a, ba_of(0, 1)), (a, ba_of(0, 3))
    xn = (a, ba_of(1, 0))

    tile_copy = pltpu.make_async_copy(tiles_hbm, tiles.at[pl.ds(0, 128)], loc_sem.at[0])
    tile_copy.start()
    w2_copies = []
    for f in range(NB):
        w2_copies.append(
            pltpu.make_async_copy(
                w2_hbm.at[:, pl.ds(f * TILE, TILE)],
                w2c.at[f],
                loc_sem.at[1 + f],
            )
        )
        w2_copies[-1].start()

    barrier = pltpu.get_barrier_semaphore()
    for k in range(1, 8):
        pl.semaphore_signal(barrier, inc=1, device_id=(aa_of(k // 2, k % 2), b), device_id_type=MESH)
    for peer in (sibling, zp, zm, xn):
        pl.semaphore_signal(barrier, inc=1, device_id=peer, device_id_type=MESH)

    tiles[128] = jnp.zeros((TILE, TILE), BF)
    feats[pl.ds(a * 4, 4)] = x_ref[...].reshape(4, TILE, TILE)

    prepare(row_ref[...], col_ref[...], index_v, keep_v)
    index_copy = pltpu.make_async_copy(index_v, index, loc_sem.at[9])
    keep_copy = pltpu.make_async_copy(keep_v, keeps, loc_sem.at[10])
    index_copy.start()
    keep_copy.start()
    pl.semaphore_wait(barrier, 11)

    def gather(buf, s_sem, r_sem, s_fwd, r_fwd, use):
        def block(owner):
            return buf.at[pl.ds(owner * 4, 4)]

        def to_peer(k):
            peer = aa_of(k // 2, lax.rem(k, 2))
            return pltpu.make_async_remote_copy(
                src_ref=block(a), dst_ref=block(a), send_sem=s_sem.at[k], recv_sem=r_sem.at[k],
                device_id=(peer, b), device_id_type=MESH,
            )

        def forward(k):
            owner = aa_of(4 - k // 2, lax.rem(k, 2))
            return pltpu.make_async_remote_copy(
                src_ref=block(owner), dst_ref=block(owner), send_sem=s_fwd.at[k], recv_sem=r_fwd.at[k],
                device_id=sibling, device_id_type=MESH,
            )

        for k in (1, 6, 2, 7, 3, 4, 5):
            to_peer(k).start()
        forward(0).start()

        def arrive(k):
            to_peer(k).wait_recv()
            forward(k).start()

        def owners(dy, same):
            here = aa_of(dy, 0), aa_of(dy, 1)
            return here if same else tuple(o + 1 - 2 * c for o in here)

        def siblings(dy):
            forward((8 - 2 * dy) % 8).wait_recv()
            forward((8 - 2 * dy) % 8 + 1).wait_recv()
            if use is not None:
                use(*owners(dy, False))

        before = None
        for dy in (0, 1, 3, 2):
            if dy > 0:
                arrive(8 - 2 * dy)
            arrive((8 - 2 * dy) % 8 + 1)
            if use is not None:
                use(*owners(dy, True))
            if before is not None:
                siblings(before)
            before = dy
        siblings(before)

        def finish():
            def body(k, carry):
                to_peer(k).wait_send()
                forward(k).wait_send()
                return carry

            lax.fori_loop(1, 8, body, 0)
            forward(0).wait_send()

        return finish

    finish_a = gather(feats, as_sem, ar_sem, fs_sem, fr_sem, None)
    tile_copy.wait()
    index_copy.wait()
    keep_copy.wait()

    group = 16

    def pair_products(source, offset, width, acc, store):
        acc[:, pl.ds(0, width)] = jnp.zeros((TILE, width), F32)

        def body(i, carry):
            running = acc[:, pl.ds(0, width)]
            for j in range(group):
                q = i * group + j
                left = jnp.concatenate([tiles[index[0, 2 * q]], tiles[index[0, 2 * q + 1]]], axis=1)
                cols = pl.ds(offset, width)
                right = jnp.concatenate([source[index[1, 2 * q], :, cols], source[index[1, 2 * q + 1], :, cols]], axis=0)
                running = running * keeps[0, q] + jnp.dot(left, right, preferred_element_type=F32)
                store(q, running)
            acc[:, pl.ds(0, width)] = running
            return carry

        lax.fori_loop(0, PAIRS // group, body, 0)

    def each(count, body):
        def one(i, carry):
            body(i)
            return carry

        lax.fori_loop(0, count, one, 0)

    def layer_one(sums1, acc, cs):
        sums1[PAIRS] = jnp.zeros((TILE, TILE), F32)

        def store1(q, value):
            sums1[q] = value

        pair_products(feats, 0, TILE, acc, store1)

        def own(dx, dz, j):
            return sums1[index[2, ba_of(dx, dz) * 4 + j]]

        def message(i, offset, count, peer):
            return pltpu.make_async_remote_copy(
                src_ref=cs.at[pl.ds(offset, count)], dst_ref=cr.at[pl.ds(offset, count)],
                send_sem=cs_sem.at[i], recv_sem=cr_sem.at[i], device_id=peer, device_id_type=MESH,
            )

        m0p, m0m = message(0, C_M0P, 2, zp), message(1, C_M0M, 2, zm)
        xsa, xsb = message(2, C_XS, 2, xn), message(3, C_XS + 2, 6, xn)
        m1pb, m1ma = message(4, C_M1P + 2, 2, zp), message(5, C_M1M, 2, zm)
        m1pa, m1mb = message(6, C_M1P, 2, zp), message(7, C_M1M + 2, 2, zm)
        t2p, t2m = message(8, C_T2, 1, zp), message(9, C_T2 + 1, 1, zm)
        t1b, t3a = message(10, C_T1 + 1, 1, zp), message(11, C_T3, 1, zm)
        t1a, t3b = message(12, C_T1, 1, zp), message(13, C_T3 + 1, 1, zm)
        xf = message(14, C_XF, 2, xn)

        for dx in range(2):
            cs[C_M0P + dx] = own(dx, 2, 0)
            cs[C_M0M + dx] = own(dx, 2, 1)
        m0p.start()
        m0m.start()
        for j in range(2):
            cs[C_XS + j] = own(1, 2, 2 + j)
        xsa.start()
        for j in range(2):
            cs[C_XS + 2 + j] = own(1, 1, 2 + j)
            cs[C_XS + 4 + j] = own(1, 3, 2 + j)
            cs[C_XS + 6 + j] = own(1, 0, 2 + j)
        xsb.start()
        for dx in range(2):
            cs[C_M1P + 2 + dx] = own(dx, 1, 1)
            cs[C_M1M + dx] = own(dx, 3, 0)
        m1pb.start()
        m1ma.start()
        xsa.wait_recv()
        for j in range(2):
            cs[C_T2 + j] = own(0, 2, 2 + j) + cr[C_XS + j]
        t2p.start()
        t2m.start()
        m0p.wait_recv()
        m0m.wait_recv()
        for dx in range(2):
            cs[C_M1P + dx] = own(dx, 1, 0) + cr[C_M0P + dx]
            cs[C_M1M + 2 + dx] = own(dx, 3, 1) + cr[C_M0M + dx]
        m1pa.start()
        m1mb.start()
        xsb.wait_recv()
        cs[C_T1 + 1] = own(0, 1, 3) + cr[C_XS + 3]
        cs[C_T3] = own(0, 3, 2) + cr[C_XS + 4]
        t1b.start()
        t3a.start()
        t2p.wait_recv()
        t2m.wait_recv()
        cs[C_T1] = own(0, 1, 2) + cr[C_XS + 2] + cr[C_T2]
        cs[C_T3 + 1] = own(0, 3, 3) + cr[C_XS + 5] + cr[C_T2 + 1]
        t1a.start()
        t3b.start()
        for copy in (m1pb, m1ma, m1pa, m1mb):
            copy.wait_recv()
        for j in range(2):
            cs[C_XF + j] = own(1, 0, j) + cr[C_M1P + 2 * j + 1] + cr[C_M1M + 2 * j + 1]
        xf.start()
        for copy in (t1b, t3a, t1a, t3b):
            copy.wait_recv()
        for j in range(2):
            value = own(0, 0, 2 + j) + cr[C_XS + 6 + j] + cr[C_T1 + j] + cr[C_T3 + j]
            lows[a * 4 + 2 + j] = value.astype(BF)
        xf.wait_recv()
        for j in range(2):
            value = own(0, 0, j) + cr[C_M1P + 2 * j] + cr[C_M1M + 2 * j] + cr[C_XF + j]
            lows[a * 4 + j] = value.astype(BF)
        for copy in (m0p, m0m, xsa, xsb, m1pb, m1ma, m1pa, m1mb, t2p, t2m, t1b, t3a, t1a, t3b, xf):
            copy.wait_send()

    pl.run_scoped(
        layer_one,
        pltpu.VMEM((PAIRS + 1, TILE, TILE), F32),
        pltpu.VMEM((TILE, TILE), F32),
        pltpu.VMEM((C_BLOCKS, TILE, TILE), F32),
    )
    finish_a()


    def message(i, offset, count, peer):
        return pltpu.make_async_remote_copy(
            src_ref=sb.at[pl.ds(offset, count)], dst_ref=rb.at[pl.ds(offset, count)],
            send_sem=es_sem.at[i], recv_sem=er_sem.at[i], device_id=peer, device_id_type=MESH,
        )

    m0p, m0m = message(0, M0P, N1, zp), message(1, M0M, N1, zm)
    xs2 = message(2, XS + 2 * N2, N2, xn)
    m1pb, m1ma = message(3, M1P + H1, H1, zp), message(4, M1M, H1, zm)
    xs1, xs3 = message(5, XS + N2, N2, xn), message(6, XS + 3 * N2, N2, xn)
    t2p, t2m = message(7, T2, H2, zp), message(8, T2 + H2, H2, zm)
    m1pa, m1mb = message(9, M1P, H1, zp), message(10, M1M + H1, H1, zm)
    m2p, m2m = message(11, M2P, N1, zp), message(12, M2M, N1, zm)
    t1b, t3a = message(13, T1 + H2, H2, zp), message(14, T3, H2, zm)
    t1a, t3b = message(15, T1, H2, zp), message(16, T3 + H2, H2, zm)
    xs0 = message(17, XS, N2, xn)
    xfa, xfb = message(18, XF, H1, xn), message(19, XF + H1, H1, xn)
    messages = [m0p, m0m, xs2, m1pb, m1ma, xs1, xs3, t2p, t2m, m1pa, m1mb, m2p, m2m, t1b, t3a, t1a, t3b, xs0, xfa, xfb]

    def layer_two(hid, proj, sums2, acc):
        sums2[PAIRS] = jnp.zeros((TILE, 2 * TILE), BF)

        def columns(half):
            places = (((0, 2), (1, 2), (1, 1), (1, 3)), ((0, 1), (0, 3), (0, 0), (1, 0)))[half]
            return jnp.concatenate([w2c[ba_of(dx, dz)] for dx, dz in places], axis=1)

        def project(rows, half):
            return jnp.dot(rows, columns(half), preferred_element_type=F32).astype(BF)

        def hidden_of(one, two):
            rows = [lows[pl.ds(o * 4, 4)].reshape(4 * TILE, TILE) for o in (one, two)]
            value = jnp.dot(jnp.concatenate(rows, axis=0), w1_ref[...], preferred_element_type=F32) + b1_ref[...]
            value = jnp.maximum(value, 0.0).astype(BF)
            hid[one] = value[: 4 * TILE]
            hid[two] = value[4 * TILE :]
            value = project(value, 0).reshape(8, TILE, 4 * TILE)
            proj[pl.ds(one * 4, 4)] = value[:4]
            proj[pl.ds(two * 4, 4)] = value[4:]

        finish_d = gather(lows, ds_sem, dr_sem, gs_sem, gr_sem, hidden_of)
        finish_d()

        def store2(q, value):
            sums2[q] = value.astype(BF)

        def pick(r):
            value = sums2[index[2, r]].astype(F32)
            return value[:, :TILE], value[:, TILE:]

        def got(i):
            return rb[i].astype(F32)

        def put(i, value):
            sb[i] = value.astype(BF)

        pair_products(proj, 0 * TILE, 2 * TILE, acc, store2)

        def body(i):
            near, far = pick(i)
            put(M0P + i, near)
            put(M0P + H1 + i, far)
            near, far = pick(H1 + i)
            put(M0M + i, near)
            put(M0M + H1 + i, far)

        each(H1, body)
        m0p.start()
        m0m.start()

        def body(i):
            near, far = pick(N1 + i)
            put(T2 + i, near)
            put(XS + 2 * N2 + i, far)

        each(N2, body)
        xs2.start()

        pair_products(proj, 2 * TILE, 2 * TILE, acc, store2)

        def body(i):
            plus, minus = pick(N1 + i)
            put(XS + N2 + i, plus)
            put(XS + 3 * N2 + i, minus)

        each(N2, body)
        xs1.start()
        xs3.start()

        def body(i):
            put(M1M + i, pick(i)[1])
            put(M1P + H1 + i, pick(H1 + i)[0])

        each(H1, body)
        m1pb.start()
        m1ma.start()

        def body(i):
            rows = hid[pl.ds(2 * i, 2)].reshape(8 * TILE, 1024)
            proj[pl.ds(8 * i, 8)] = project(rows, 1).reshape(8, TILE, 4 * TILE)

        each(NA // 2, body)
        m0p.wait_recv()
        m0m.wait_recv()

        def body(i):
            put(M1P + i, pick(i)[0] + got(M0P + H1 + i))
            put(M1M + H1 + i, pick(H1 + i)[1] + got(M0M + H1 + i))

        each(H1, body)
        m1pa.start()
        m1mb.start()
        xs2.wait_recv()

        def body(i):
            put(T2 + i, sb[T2 + i].astype(F32) + got(XS + 2 * N2 + i))

        each(N2, body)
        t2p.start()
        t2m.start()

        pair_products(proj, 0 * TILE, 2 * TILE, acc, store2)

        def body(i):
            plus, minus = pick(i)
            put(M2P + i, plus + got(M0P + i))
            put(M2M + i, minus)
            plus, minus = pick(H1 + i)
            put(M2P + H1 + i, plus)
            put(M2M + H1 + i, minus + got(M0M + i))

        each(H1, body)
        m2p.start()
        m2m.start()
        xs1.wait_recv()
        xs3.wait_recv()

        def body(i):
            plus, minus = pick(N1 + i)
            put(T1 + i, plus + got(XS + N2 + i))
            put(T3 + i, minus + got(XS + 3 * N2 + i))

        each(N2, body)
        t1b.start()
        t3a.start()

        t2p.wait_recv()
        t2m.wait_recv()

        def body(i):
            put(T1 + i, sb[T1 + i].astype(F32) + got(T2 + i))
            put(T3 + H2 + i, sb[T3 + H2 + i].astype(F32) + got(T2 + H2 + i))

        each(H2, body)
        t1a.start()
        t3b.start()

        pair_products(proj, 2 * TILE, 2 * TILE, acc, store2)

        def body(i):
            put(XS + i, pick(N1 + i)[1])

        each(N2, body)
        xs0.start()
        m1pb.wait_recv()
        m1ma.wait_recv()
        m1pa.wait_recv()
        m1mb.wait_recv()

        def body(i):
            put(XF + i, pick(i)[1] + got(M1P + i) + got(M1M + i))

        each(H1, body)
        xfa.start()

        def body(i):
            j = H1 + i
            put(XF + j, pick(j)[1] + got(M1P + j) + got(M1M + j))

        each(H1, body)
        xfb.start()

        def write(r, value):
            out_ref[pl.ds(pl.multiple_of(r * TILE, TILE), TILE), :] = value.astype(BF)

        xs0.wait_recv()
        t1b.wait_recv()
        t1a.wait_recv()
        t3a.wait_recv()
        t3b.wait_recv()

        def body(i):
            write(N1 + i, pick(N1 + i)[0] + got(XS + i) + got(T1 + i) + got(T3 + i))

        each(N2, body)
        m2p.wait_recv()
        m2m.wait_recv()
        for start, copy in ((0, xfa), (H1, xfb)):
            copy.wait_recv()

            def body(i):
                j = start + i
                write(j, pick(j)[0] + got(M2P + j) + got(M2M + j) + got(XF + j))

            each(H1, body)
        for copy in messages:
            copy.wait_send()

    for copy in w2_copies:
        copy.wait()
    pl.run_scoped(
        layer_two,
        pltpu.VMEM((NA, 4 * TILE, 1024), BF),
        pltpu.VMEM((64, TILE, 4 * TILE), BF),
        pltpu.VMEM((PAIRS + 1, TILE, 2 * TILE), BF),
        pltpu.VMEM((TILE, 2 * TILE), F32),
    )


def on_device(features, tile_values, tile_row, tile_col, weight_one, bias_one, weight_two):
    vmem = pl.BlockSpec(memory_space=pltpu.VMEM)
    hbm = pl.BlockSpec(memory_space=pl.ANY)
    dma = pltpu.SemaphoreType.DMA
    return pl.pallas_call(
        kernel,
        out_shape=jax.ShapeDtypeStruct((RB * TILE, TILE), BF),
        in_specs=[vmem, vmem, vmem, hbm, vmem, vmem, hbm],
        out_specs=vmem,
        scratch_shapes=[
            pltpu.VMEM((129, TILE, TILE), BF),
            pltpu.VMEM((NB, 1024, TILE), BF),
            pltpu.VMEM((64, TILE, TILE), BF),
            pltpu.VMEM((C_BLOCKS, TILE, TILE), F32),
            pltpu.VMEM((64, TILE, TILE), BF),
            pltpu.VMEM((BLOCKS, TILE, TILE), BF),
            pltpu.VMEM((BLOCKS, TILE, TILE), BF),
            pltpu.VMEM((8, 2 * TILE), jnp.int32),
            pltpu.VMEM((8, TILE), F32),
            pltpu.SMEM((8, 2 * TILE), jnp.int32),
            pltpu.SMEM((8, TILE), F32),
        ]
        + [dma((11,))]
        + [dma((8,))] * 4
        + [dma((15,))] * 2
        + [dma((8,))] * 4
        + [dma((20,))] * 2,
        compiler_params=pltpu.CompilerParams(
            collective_id=0, has_side_effects=True, vmem_limit_bytes=64 * 2**20 - 2**16
        ),
        cost_estimate=pl.CostEstimate(flops=26 * 10**9, bytes_accessed=8 * 2**20, transcendentals=0),
        name="two_layers",
    )(tile_row.reshape(1, -1), tile_col.reshape(1, -1), features, tile_values, weight_one, bias_one.reshape(1, -1), weight_two)


def solution(mesh):
    return jax.shard_map(
        on_device,
        mesh=mesh,
        in_specs=(
            P(("aa", "ba"), None),
            P(("aa", "ba"), None, None),
            P(("aa", "ba")),
            P(("aa", "ba")),
            P(),
            P(),
            P(),
        ),
        out_specs=P("aa", "ba"),
        check_vma=False,
    )
```

time: 163 us -> 130 us (0.80)
  Pallas kernels: 156 us -> 128 us
  other arithmetic: 4.29 us -> 0 us
    pallas_call x1, Pallas kernels: 156 us -> 128 us  [on_device(): pl.pallas_call(kernel, out_shape=jax.ShapeDtypeStruct((RB * TILE, TILE),...]
    select_n x4 -> x0, other arithmetic: 1.89 us -> none  [the longest x1 0.69 us: prepare(): jnp.where(row >= 0, 2 * jnp.sum(jnp.where(hot, start[None, :], 0), axis=1...]
where the time goes in v2:
time: 130 us
  Pallas kernels  128 us (98%)
  local copies, waits for them, and re-layouts  2.26 us (2%)
    pallas_call x1, Pallas kernels, on_device(): pl.pallas_call(kernel, out_shape=jax.ShapeDtypeStruct((RB * TILE, TILE),...  128 us

profile of v2, /device:TPU:0, one launch (start us, length us, event | category | flops | bytes accessed | tf_op | source)
XLA Modules:
  0.0 130.0 jit_solution(4966008844986754774)
XLA Ops:
  0.0 127.7 %two_layers.1 = bf16[4096,128]{1,0:T(8,128)(2,1)} custom-call(s32[1,128]{1,0:T(1,128)} %bitcast.4, s32[1,128]{1,0:T(1,128)} %bitcast.5, bf16[512,128]{1,0:T(8,128)(2,1)} %x_ref.1, bf16[128,128,128]{2,1,0:T(8,128)(2,1)} %tiles_hbm.1, bf16[128,1024]{1,0:T(8,128)(2,1)} %w1_ref.1, f32[1,1024]{1,0:T(1,128)} %bitcast.3, bf16[1024,1024]{1,0:T(8,128)(2,1)} %w2_hbm.1), custom_call_target="tpu_custom_call" | custom-call | flops 25999998976 | bytes 8388608 | tf_op jit(solution)/shard_map/two_layers/pallas_call | solution.py:529
  127.7 2.3 %copy.9 = bf16[4096,128]{1,0:T(8,128)(2,1)} copy(bf16[4096,128]{1,0:T(8,128)(2,1)} %two_layers.1) | data formatting | bytes 2097152

commit v3 on v2

--- a/solution.py
+++ b/solution.py
@@ -74,8 +74,8 @@
 
 
 def kernel(
-    row_ref, col_ref, x_ref, tiles_hbm, w1_ref, b1_ref, w2_hbm, out_ref,
-    tiles, w2c, feats, cr, lows, sb, rb, index_v, keep_v, index, keeps,
+    row_hbm, col_hbm, x_hbm, tiles_hbm, w1_hbm, b1_hbm, w2_hbm, out_hbm,
+    tiles, w2c, feats, cr, lows, sb, rb, index_v, keep_v, index, keeps, row_ref, col_ref, w1_ref, b1_ref, out_ref,
     loc_sem, as_sem, ar_sem, fs_sem, fr_sem, cs_sem, cr_sem, ds_sem, dr_sem, gs_sem, gr_sem, es_sem, er_sem,
 ):
     a, b = lax.axis_index("aa"), lax.axis_index("ba")
@@ -92,6 +92,23 @@
     zp, zm = (a, ba_of(0, 1)), (a, ba_of(0, 3))
     xn = (a, ba_of(1, 0))
 
+    barrier = pltpu.get_barrier_semaphore()
+    for k in (4, 1, 2, 6):
+        pl.semaphore_signal(barrier, inc=1, device_id=(aa_of(k // 2, k % 2), b), device_id_type=MESH)
+    for peer in (sibling, zp, zm, xn):
+        pl.semaphore_signal(barrier, inc=1, device_id=peer, device_id_type=MESH)
+
+    early = [
+        pltpu.make_async_copy(x_hbm, feats.at[pl.ds(a * 4, 4)], loc_sem.at[11]),
+        pltpu.make_async_copy(row_hbm, row_ref, loc_sem.at[12]),
+        pltpu.make_async_copy(col_hbm, col_ref, loc_sem.at[13]),
+    ]
+    late = [
+        pltpu.make_async_copy(w1_hbm, w1_ref, loc_sem.at[14]),
+        pltpu.make_async_copy(b1_hbm, b1_ref, loc_sem.at[15]),
+    ]
+    for copy in early + late:
+        copy.start()
     tile_copy = pltpu.make_async_copy(tiles_hbm, tiles.at[pl.ds(0, 128)], loc_sem.at[0])
     tile_copy.start()
     w2_copies = []
@@ -105,32 +122,29 @@
         )
         w2_copies[-1].start()
 
-    barrier = pltpu.get_barrier_semaphore()
-    for k in range(1, 8):
-        pl.semaphore_signal(barrier, inc=1, device_id=(aa_of(k // 2, k % 2), b), device_id_type=MESH)
-    for peer in (sibling, zp, zm, xn):
-        pl.semaphore_signal(barrier, inc=1, device_id=peer, device_id_type=MESH)
-
     tiles[128] = jnp.zeros((TILE, TILE), BF)
-    feats[pl.ds(a * 4, 4)] = x_ref[...].reshape(4, TILE, TILE)
-
-    prepare(row_ref[...], col_ref[...], index_v, keep_v)
-    index_copy = pltpu.make_async_copy(index_v, index, loc_sem.at[9])
-    keep_copy = pltpu.make_async_copy(keep_v, keeps, loc_sem.at[10])
-    index_copy.start()
-    keep_copy.start()
-    pl.semaphore_wait(barrier, 11)
-
-    def gather(buf, s_sem, r_sem, s_fwd, r_fwd, use):
+
+    early[0].wait()
+    pl.semaphore_wait(barrier, 8)
+
+    def gather(buf, s_sem, r_sem, s_fwd, r_fwd, use, between=None):
         def block(owner):
             return buf.at[pl.ds(owner * 4, 4)]
 
-        def to_peer(k):
-            peer = aa_of(k // 2, lax.rem(k, 2))
+        def remote(i, ref, peer):
             return pltpu.make_async_remote_copy(
-                src_ref=block(a), dst_ref=block(a), send_sem=s_sem.at[k], recv_sem=r_sem.at[k],
+                src_ref=ref, dst_ref=ref, send_sem=s_sem.at[i], recv_sem=r_sem.at[i],
                 device_id=(peer, b), device_id_type=MESH,
             )
+
+        def to_peer(k):
+            return remote(k, block(a), aa_of(k // 2, k % 2))
+
+        def first_half(dy):
+            return remote(2 * dy + 1, buf.at[pl.ds(aa_of(0, 1) * 4, 2)], aa_of(dy, 0))
+
+        def second_half(dy):
+            return remote(8 + dy, buf.at[pl.ds(aa_of(4 - dy, 0) * 4 + 2, 2)], aa_of(0, 1))
 
         def forward(k):
             owner = aa_of(4 - k // 2, lax.rem(k, 2))
@@ -139,48 +153,72 @@
                 device_id=sibling, device_id_type=MESH,
             )
 
-        for k in (1, 6, 2, 7, 3, 4, 5):
+        for k in (1, 6, 2, 4):
             to_peer(k).start()
         forward(0).start()
 
-        def arrive(k):
-            to_peer(k).wait_recv()
-            forward(k).start()
-
-        def owners(dy, same):
-            here = aa_of(dy, 0), aa_of(dy, 1)
-            return here if same else tuple(o + 1 - 2 * c for o in here)
-
-        def siblings(dy):
-            forward((8 - 2 * dy) % 8).wait_recv()
-            forward((8 - 2 * dy) % 8 + 1).wait_recv()
+        if between is not None:
+            between()
+
+        def own(k, l):
             if use is not None:
-                use(*owners(dy, False))
-
-        before = None
-        for dy in (0, 1, 3, 2):
-            if dy > 0:
-                arrive(8 - 2 * dy)
-            arrive((8 - 2 * dy) % 8 + 1)
+                use(aa_of(4 - k // 2, k % 2), aa_of(4 - l // 2, l % 2))
+
+        def other(k, l):
+            forward(k).wait_recv()
+            forward(l).wait_recv()
             if use is not None:
-                use(*owners(dy, True))
-            if before is not None:
-                siblings(before)
-            before = dy
-        siblings(before)
+                use(aa_of(4 - k // 2, k % 2) + 1 - 2 * c, aa_of(4 - l // 2, l % 2) + 1 - 2 * c)
+
+        to_peer(1).wait_recv()
+        for dy in (2, 1, 3):
+            first_half(dy).start()
+        forward(1).start()
+        own(0, 1)
+        for dy in (1, 3):
+            to_peer(2 * dy).wait_recv()
+            second_half(dy).start()
+            forward(2 * dy).start()
+        own(2, 6)
+        to_peer(4).wait_recv()
+        second_half(2).start()
+        forward(4).start()
+        other(0, 1)
+        other(2, 6)
+        for dy in (1, 3):
+            first_half(dy).wait_recv()
+            second_half(dy).wait_recv()
+            forward(2 * dy + 1).start()
+        own(4, 3)
+        first_half(2).wait_recv()
+        second_half(2).wait_recv()
+        forward(5).start()
+        own(7, 5)
+        other(4, 3)
+        other(7, 5)
 
         def finish():
-            def body(k, carry):
+            for k in (1, 2, 4, 6):
                 to_peer(k).wait_send()
+            for dy in (1, 2, 3):
+                first_half(dy).wait_send()
+                second_half(dy).wait_send()
+            for k in range(8):
                 forward(k).wait_send()
-                return carry
-
-            lax.fori_loop(1, 8, body, 0)
-            forward(0).wait_send()
 
         return finish
 
-    finish_a = gather(feats, as_sem, ar_sem, fs_sem, fr_sem, None)
+    index_copy = pltpu.make_async_copy(index_v, index, loc_sem.at[9])
+    keep_copy = pltpu.make_async_copy(keep_v, keeps, loc_sem.at[10])
+
+    def order():
+        early[1].wait()
+        early[2].wait()
+        prepare(row_ref[...], col_ref[...], index_v, keep_v)
+        index_copy.start()
+        keep_copy.start()
+
+    finish_a = gather(feats, as_sem, ar_sem, fs_sem, fr_sem, None, order)
     tile_copy.wait()
     index_copy.wait()
     keep_copy.wait()
@@ -317,21 +355,28 @@
     t2p, t2m = message(7, T2, H2, zp), message(8, T2 + H2, H2, zm)
     m1pa, m1mb = message(9, M1P, H1, zp), message(10, M1M + H1, H1, zm)
     m2p, m2m = message(11, M2P, N1, zp), message(12, M2M, N1, zm)
-    t1b, t3a = message(13, T1 + H2, H2, zp), message(14, T3, H2, zm)
-    t1a, t3b = message(15, T1, H2, zp), message(16, T3 + H2, H2, zm)
-    xs0 = message(17, XS, N2, xn)
-    xfa, xfb = message(18, XF, H1, xn), message(19, XF + H1, H1, xn)
-    messages = [m0p, m0m, xs2, m1pb, m1ma, xs1, xs3, t2p, t2m, m1pa, m1mb, m2p, m2m, t1b, t3a, t1a, t3b, xs0, xfa, xfb]
+    t1, t3 = message(13, T1, N2, zp), message(14, T3, N2, zm)
+    xs0 = message(15, XS, N2, xn)
+    xfa, xfb = message(16, XF, H1, xn), message(17, XF + H1, H1, xn)
+    messages = [m0p, m0m, xs2, m1pb, m1ma, xs1, xs3, t2p, t2m, m1pa, m1mb, m2p, m2m, t1, t3, xs0, xfa, xfb]
 
     def layer_two(hid, proj, sums2, acc):
         sums2[PAIRS] = jnp.zeros((TILE, 2 * TILE), BF)
 
-        def columns(half):
-            places = (((0, 2), (1, 2), (1, 1), (1, 3)), ((0, 1), (0, 3), (0, 0), (1, 0)))[half]
+        def columns(s):
+            places = (((0, 2), (1, 2)), ((1, 1), (1, 3)), ((0, 1), (0, 3)), ((0, 0), (1, 0)))[s]
             return jnp.concatenate([w2c[ba_of(dx, dz)] for dx, dz in places], axis=1)
 
-        def project(rows, half):
-            return jnp.dot(rows, columns(half), preferred_element_type=F32).astype(BF)
+        def project(rows, s):
+            return jnp.dot(rows, columns(s), preferred_element_type=F32).astype(BF)
+
+        def project_all(s):
+            def body(i):
+                rows = hid[pl.ds(4 * i, 4)].reshape(16 * TILE, 1024)
+                value = project(rows, s).reshape(16, TILE, 2 * TILE)
+                proj[pl.ds(16 * i, 16), :, pl.ds(s % 2 * 2 * TILE, 2 * TILE)] = value
+
+            each(NA // 4, body)
 
         def hidden_of(one, two):
             rows = [lows[pl.ds(o * 4, 4)].reshape(4 * TILE, TILE) for o in (one, two)]
@@ -339,9 +384,9 @@
             value = jnp.maximum(value, 0.0).astype(BF)
             hid[one] = value[: 4 * TILE]
             hid[two] = value[4 * TILE :]
-            value = project(value, 0).reshape(8, TILE, 4 * TILE)
-            proj[pl.ds(one * 4, 4)] = value[:4]
-            proj[pl.ds(two * 4, 4)] = value[4:]
+            value = project(value, 0).reshape(8, TILE, 2 * TILE)
+            proj[pl.ds(one * 4, 4), :, pl.ds(0, 2 * TILE)] = value[:4]
+            proj[pl.ds(two * 4, 4), :, pl.ds(0, 2 * TILE)] = value[4:]
 
         finish_d = gather(lows, ds_sem, dr_sem, gs_sem, gr_sem, hidden_of)
         finish_d()
@@ -381,6 +426,8 @@
         each(N2, body)
         xs2.start()
 
+        project_all(1)
+
         pair_products(proj, 2 * TILE, 2 * TILE, acc, store2)
 
         def body(i):
@@ -400,11 +447,7 @@
         m1pb.start()
         m1ma.start()
 
-        def body(i):
-            rows = hid[pl.ds(2 * i, 2)].reshape(8 * TILE, 1024)
-            proj[pl.ds(8 * i, 8)] = project(rows, 1).reshape(8, TILE, 4 * TILE)
-
-        each(NA // 2, body)
+        project_all(2)
         m0p.wait_recv()
         m0m.wait_recv()
 
@@ -437,28 +480,14 @@
         each(H1, body)
         m2p.start()
         m2m.start()
-        xs1.wait_recv()
-        xs3.wait_recv()
 
         def body(i):
             plus, minus = pick(N1 + i)
-            put(T1 + i, plus + got(XS + N2 + i))
-            put(T3 + i, minus + got(XS + 3 * N2 + i))
+            put(T1 + i, plus)
+            put(T3 + i, minus)
 
         each(N2, body)
-        t1b.start()
-        t3a.start()
-
-        t2p.wait_recv()
-        t2m.wait_recv()
-
-        def body(i):
-            put(T1 + i, sb[T1 + i].astype(F32) + got(T2 + i))
-            put(T3 + H2 + i, sb[T3 + H2 + i].astype(F32) + got(T2 + H2 + i))
-
-        each(H2, body)
-        t1a.start()
-        t3b.start()
+        project_all(3)
 
         pair_products(proj, 2 * TILE, 2 * TILE, acc, store2)
 
@@ -485,22 +514,40 @@
         each(H1, body)
         xfb.start()
 
+        for copy in (xs1, xs3, t2p, t2m):
+            copy.wait_recv()
+
+        def body(i):
+            j = H2 + i
+            put(T1 + i, sb[T1 + i].astype(F32) + got(XS + N2 + i) + got(T2 + i))
+            put(T1 + j, sb[T1 + j].astype(F32) + got(XS + N2 + j))
+            put(T3 + i, sb[T3 + i].astype(F32) + got(XS + 3 * N2 + i))
+            put(T3 + j, sb[T3 + j].astype(F32) + got(XS + 3 * N2 + j) + got(T2 + j))
+
+        each(H2, body)
+        t1.start()
+        t3.start()
+
         def write(r, value):
-            out_ref[pl.ds(pl.multiple_of(r * TILE, TILE), TILE), :] = value.astype(BF)
+            out_ref[r] = value.astype(BF)
+
+        def flush(i, start, count):
+            return pltpu.make_async_copy(out_ref.at[pl.ds(start, count)], out_hbm.at[pl.ds(start, count)], loc_sem.at[16 + i])
+
+        flushes = [flush(0, N1, N2), flush(1, 0, H1), flush(2, H1, H1)]
 
         xs0.wait_recv()
-        t1b.wait_recv()
-        t1a.wait_recv()
-        t3a.wait_recv()
-        t3b.wait_recv()
+        t1.wait_recv()
+        t3.wait_recv()
 
         def body(i):
             write(N1 + i, pick(N1 + i)[0] + got(XS + i) + got(T1 + i) + got(T3 + i))
 
         each(N2, body)
+        flushes[0].start()
         m2p.wait_recv()
         m2m.wait_recv()
-        for start, copy in ((0, xfa), (H1, xfb)):
+        for start, copy, copy_out in ((0, xfa, flushes[1]), (H1, xfb, flushes[2])):
             copy.wait_recv()
 
             def body(i):
@@ -508,10 +555,13 @@
                 write(j, pick(j)[0] + got(M2P + j) + got(M2M + j) + got(XF + j))
 
             each(H1, body)
+            copy_out.start()
         for copy in messages:
             copy.wait_send()
-
-    for copy in w2_copies:
+        for copy_out in flushes:
+            copy_out.wait()
+
+    for copy in w2_copies + late:
         copy.wait()
     pl.run_scoped(
         layer_two,
@@ -523,14 +573,13 @@
 
 
 def on_device(features, tile_values, tile_row, tile_col, weight_one, bias_one, weight_two):
-    vmem = pl.BlockSpec(memory_space=pltpu.VMEM)
     hbm = pl.BlockSpec(memory_space=pl.ANY)
     dma = pltpu.SemaphoreType.DMA
     return pl.pallas_call(
         kernel,
-        out_shape=jax.ShapeDtypeStruct((RB * TILE, TILE), BF),
-        in_specs=[vmem, vmem, vmem, hbm, vmem, vmem, hbm],
-        out_specs=vmem,
+        out_shape=jax.ShapeDtypeStruct((RB, TILE, TILE), BF),
+        in_specs=[hbm] * 7,
+        out_specs=hbm,
         scratch_shapes=[
             pltpu.VMEM((129, TILE, TILE), BF),
             pltpu.VMEM((NB, 1024, TILE), BF),
@@ -543,18 +592,23 @@
             pltpu.VMEM((8, TILE), F32),
             pltpu.SMEM((8, 2 * TILE), jnp.int32),
             pltpu.SMEM((8, TILE), F32),
+            pltpu.VMEM((1, TILE), jnp.int32),
+            pltpu.VMEM((1, TILE), jnp.int32),
+            pltpu.VMEM((TILE, 1024), BF),
+            pltpu.VMEM((1, 1024), F32),
+            pltpu.VMEM((RB, TILE, TILE), BF),
         ]
-        + [dma((11,))]
-        + [dma((8,))] * 4
+        + [dma((19,))]
+        + [dma((12,))] * 4
         + [dma((15,))] * 2
-        + [dma((8,))] * 4
-        + [dma((20,))] * 2,
+        + [dma((12,))] * 4
+        + [dma((18,))] * 2,
         compiler_params=pltpu.CompilerParams(
             collective_id=0, has_side_effects=True, vmem_limit_bytes=64 * 2**20 - 2**16
         ),
         cost_estimate=pl.CostEstimate(flops=26 * 10**9, bytes_accessed=8 * 2**20, transcendentals=0),
         name="two_layers",
-    )(tile_row.reshape(1, -1), tile_col.reshape(1, -1), features, tile_values, weight_one, bias_one.reshape(1, -1), weight_two)
+    )(tile_row.reshape(1, -1), tile_col.reshape(1, -1), features.reshape(4, TILE, TILE), tile_values, weight_one, bias_one.reshape(1, -1), weight_two).reshape(RB * TILE, TILE)
 
 
 def solution(mesh):

time: 130 us -> 121 us (0.931)
  Pallas kernels: 128 us -> 118 us
    pallas_call x1, Pallas kernels: 128 us -> 118 us  [on_device(): pl.pallas_call(kernel, out_shape=jax.ShapeDtypeStruct((RB, TILE, TILE), B...]
where the time goes in v3:
time: 121 us
  Pallas kernels  118 us (98%)
  local copies, waits for them, and re-layouts  2.26 us (2%)
    pallas_call x1, Pallas kernels, on_device(): pl.pallas_call(kernel, out_shape=jax.ShapeDtypeStruct((RB, TILE, TILE), B...  118 us

profile of v3, /device:TPU:0, one launch (start us, length us, event | category | flops | bytes accessed | tf_op | source)
XLA Modules:
  0.0 120.5 jit_solution(6508271811236462795)
XLA Ops:
  0.0 118.2 %two_layers.1 = bf16[32,128,128]{2,1,0:T(8,128)(2,1)} custom-call(s32[1,128]{1,0:T(1,128)} %bitcast.8, s32[1,128]{1,0:T(1,128)} %bitcast.9, bf16[4,128,128]{2,1,0:T(8,128)(2,1)} %bitcast.6, bf16[128,128,128]{2,1,0:T(8,128)(2,1)} %tiles_hbm.1, bf16[128,1024]{1,0:T(8,128)(2,1)} %w1_hbm.1, f32[1,1024]{1,0:T(1,128)} %bitcast.7, bf16[1024,1024]{1,0:T(8,128)(2,1)} %w2_hbm.1), custom_call_target="tpu_custom_call" | custom-call | flops 25999998976 | bytes 8388608 | tf_op jit(solution)/shard_map/two_layers/pallas_call | solution.py:578
  118.2 2.3 %copy.9 = bf16[4096,128]{1,0:T(8,128)(2,1)} copy(bf16[4096,128]{1,0:T(8,128)(2,1)} %bitcast.5) | data formatting | bytes 2097152

commit v4 on v3

--- a/solution.py
+++ b/solution.py
@@ -15,6 +15,7 @@
 RB = 32
 N1 = 18
 H1 = N1 // 2
+X1 = 12
 N2 = RB - N1
 H2 = N2 // 2
 M0P, M0M, M1P, M1M, M2P, M2M = 0, N1, 2 * N1, 3 * N1, 4 * N1, 5 * N1
@@ -223,7 +224,7 @@
     index_copy.wait()
     keep_copy.wait()
 
-    group = 16
+    group = 20
 
     def pair_products(source, offset, width, acc, store):
         acc[:, pl.ds(0, width)] = jnp.zeros((TILE, width), F32)
@@ -357,7 +358,7 @@
     m2p, m2m = message(11, M2P, N1, zp), message(12, M2M, N1, zm)
     t1, t3 = message(13, T1, N2, zp), message(14, T3, N2, zm)
     xs0 = message(15, XS, N2, xn)
-    xfa, xfb = message(16, XF, H1, xn), message(17, XF + H1, H1, xn)
+    xfa, xfb = message(16, XF, X1, xn), message(17, XF + X1, N1 - X1, xn)
     messages = [m0p, m0m, xs2, m1pb, m1ma, xs1, xs3, t2p, t2m, m1pa, m1mb, m2p, m2m, t1, t3, xs0, xfa, xfb]
 
     def layer_two(hid, proj, sums2, acc):
@@ -504,14 +505,14 @@
         def body(i):
             put(XF + i, pick(i)[1] + got(M1P + i) + got(M1M + i))
 
-        each(H1, body)
+        each(X1, body)
         xfa.start()
 
         def body(i):
-            j = H1 + i
+            j = X1 + i
             put(XF + j, pick(j)[1] + got(M1P + j) + got(M1M + j))
 
-        each(H1, body)
+        each(N1 - X1, body)
         xfb.start()
 
         for copy in (xs1, xs3, t2p, t2m):
@@ -534,7 +535,7 @@
         def flush(i, start, count):
             return pltpu.make_async_copy(out_ref.at[pl.ds(start, count)], out_hbm.at[pl.ds(start, count)], loc_sem.at[16 + i])
 
-        flushes = [flush(0, N1, N2), flush(1, 0, H1), flush(2, H1, H1)]
+        flushes = [flush(0, N1, N2), flush(1, 0, X1), flush(2, X1, N1 - X1)]
 
         xs0.wait_recv()
         t1.wait_recv()
@@ -547,14 +548,14 @@
         flushes[0].start()
         m2p.wait_recv()
         m2m.wait_recv()
-        for start, copy, copy_out in ((0, xfa, flushes[1]), (H1, xfb, flushes[2])):
+        for start, count, copy, copy_out in ((0, X1, xfa, flushes[1]), (X1, N1 - X1, xfb, flushes[2])):
             copy.wait_recv()
 
             def body(i):
                 j = start + i
                 write(j, pick(j)[0] + got(M2P + j) + got(M2M + j) + got(XF + j))
 
-            each(H1, body)
+            each(count, body)
             copy_out.start()
         for copy in messages:
             copy.wait_send()

time: 121 us -> 120 us (level)
  no operation moved by 1% of the time
where the time goes in v4:
time: 120 us
  Pallas kernels  118 us (98%)
  local copies, waits for them, and re-layouts  2.26 us (2%)
    pallas_call x1, Pallas kernels, on_device(): pl.pallas_call(kernel, out_shape=jax.ShapeDtypeStruct((RB, TILE, TILE), B...  118 us

profile of v4, /device:TPU:0, one launch (start us, length us, event | category | flops | bytes accessed | tf_op | source)
XLA Modules:
  0.0 120.2 jit_solution(989051939262478499)
XLA Ops:
  0.0 117.9 %two_layers.1 = bf16[32,128,128]{2,1,0:T(8,128)(2,1)} custom-call(s32[1,128]{1,0:T(1,128)} %bitcast.8, s32[1,128]{1,0:T(1,128)} %bitcast.9, bf16[4,128,128]{2,1,0:T(8,128)(2,1)} %bitcast.6, bf16[128,128,128]{2,1,0:T(8,128)(2,1)} %tiles_hbm.1, bf16[128,1024]{1,0:T(8,128)(2,1)} %w1_hbm.1, f32[1,1024]{1,0:T(1,128)} %bitcast.7, bf16[1024,1024]{1,0:T(8,128)(2,1)} %w2_hbm.1), custom_call_target="tpu_custom_call" | custom-call | flops 25999998976 | bytes 8388608 | tf_op jit(solution)/shard_map/two_layers/pallas_call | solution.py:579
  117.9 2.3 %copy.9 = bf16[4096,128]{1,0:T(8,128)(2,1)} copy(bf16[4096,128]{1,0:T(8,128)(2,1)} %bitcast.5) | data formatting | bytes 2097152

commit v5 on v4

--- a/solution.py
+++ b/solution.py
@@ -537,6 +537,19 @@
 
         flushes = [flush(0, N1, N2), flush(1, 0, X1), flush(2, X1, N1 - X1)]
 
+        def rows_of(start, count, copy, copy_out):
+            copy.wait_recv()
+
+            def body(i):
+                j = start + i
+                write(j, pick(j)[0] + got(M2P + j) + got(M2M + j) + got(XF + j))
+
+            each(count, body)
+            copy_out.start()
+
+        m2p.wait_recv()
+        m2m.wait_recv()
+        rows_of(0, X1, xfa, flushes[1])
         xs0.wait_recv()
         t1.wait_recv()
         t3.wait_recv()
@@ -546,17 +559,7 @@
 
         each(N2, body)
         flushes[0].start()
-        m2p.wait_recv()
-        m2m.wait_recv()
-        for start, count, copy, copy_out in ((0, X1, xfa, flushes[1]), (X1, N1 - X1, xfb, flushes[2])):
-            copy.wait_recv()
-
-            def body(i):
-                j = start + i
-                write(j, pick(j)[0] + got(M2P + j) + got(M2M + j) + got(XF + j))
-
-            each(count, body)
-            copy_out.start()
+        rows_of(X1, N1 - X1, xfb, flushes[2])
         for copy in messages:
             copy.wait_send()
         for copy_out in flushes:

time: 120 us -> 120 us (level)
  no operation moved by 1% of the time
where the time goes in v5:
time: 120 us
  Pallas kernels  118 us (98%)
  local copies, waits for them, and re-layouts  2.26 us (2%)
    pallas_call x1, Pallas kernels, on_device(): pl.pallas_call(kernel, out_shape=jax.ShapeDtypeStruct((RB, TILE, TILE), B...  118 us

profile of v5, /device:TPU:0, one launch (start us, length us, event | category | flops | bytes accessed | tf_op | source)
XLA Modules:
  0.0 119.9 jit_solution(999073280984321065)
XLA Ops:
  0.0 117.7 %two_layers.1 = bf16[32,128,128]{2,1,0:T(8,128)(2,1)} custom-call(s32[1,128]{1,0:T(1,128)} %bitcast.8, s32[1,128]{1,0:T(1,128)} %bitcast.9, bf16[4,128,128]{2,1,0:T(8,128)(2,1)} %bitcast.6, bf16[128,128,128]{2,1,0:T(8,128)(2,1)} %tiles_hbm.1, bf16[128,1024]{1,0:T(8,128)(2,1)} %w1_hbm.1, f32[1,1024]{1,0:T(1,128)} %bitcast.7, bf16[1024,1024]{1,0:T(8,128)(2,1)} %w2_hbm.1), custom_call_target="tpu_custom_call" | custom-call | flops 25999998976 | bytes 8388608 | tf_op jit(solution)/shard_map/two_layers/pallas_call | solution.py:582
  117.7 2.3 %copy.9 = bf16[4096,128]{1,0:T(8,128)(2,1)} copy(bf16[4096,128]{1,0:T(8,128)(2,1)} %bitcast.5) | data formatting | bytes 2097152
